TPU v7x, 512 devices: a whole 4x8x8 slice. The times are simulated.
512 devices in a mesh: band: 16 (over z, core), tile: 32 (over y, x).
Axes of the slice: x: 4, y: 8, z: 8, core: 2. Of those that a mesh axis runs over, the one named last changes fastest.
Arguments:
- sources: bfloat16 [524288, 256], P(('band', 'tile')), may hold values from -6 to 6
- observed: bfloat16 [8192, 256], P('tile'), may hold values from -6 to 6
- v_factors: bfloat16 [8, 96, 524288], P(None, None, ('band', 'tile')), may hold values from -0.1875 to 0.1875
- u_factors: bfloat16 [512, 96, 8192], P('band', None, 'tile'), may hold values from -0.03125 to 0.03125
- tile_ranks: int32 [8, 512], P(None, ('band', 'tile')), may hold values from 32 to 96
- v_exponents: int32 [8, 512], P(None, ('band', 'tile')), may hold values from -1 to 1
- u_exponents: int32 [8, 512], P(None, ('band', 'tile')), may hold values from -1 to 1
Outputs:
- residual: float32 [8192, 256], P('tile', 'band')
- gradient: bfloat16 [524288, 256], P(('band', 'tile'))
All inputs are finite; a program needn't handle non-finite values.
Results may differ from a plain program's by a relative error of at most 0.012.
Values may be sent and summed in bfloat16 or wider, within the bound.
A program may use at most 64 MiB of HBM per device.

v0:
```python
import jax
import jax.numpy as jnp
from jax import lax
from jax.sharding import PartitionSpec as P


def local(sources, observed, v_factors, u_factors, tile_ranks, v_exponents, u_exponents):
    tile_count = lax.axis_size("tile")
    band_count = lax.axis_size("band")
    row_tiles = v_factors.shape[0]
    rank_max = v_factors.shape[1]
    slices_per = tile_count // row_tiles
    rank_index = jnp.arange(rank_max, dtype=jnp.int32)
    weight = (rank_index[None, :] < tile_ranks).astype(jnp.float32)
    weight = weight * jnp.exp2((v_exponents + u_exponents).astype(jnp.float32))
    products = jnp.einsum("ikb,bs->iks", v_factors, sources, preferred_element_type=jnp.float32)
    pieces = (products * weight[:, :, None]).astype(jnp.bfloat16)
    outgoing = jnp.repeat(pieces, slices_per, axis=0)
    incoming = lax.all_to_all(outgoing, "tile", split_axis=0, concat_axis=0, tiled=True)
    partial_value = jnp.einsum(
        "ukh,uks->hs", u_factors, incoming, preferred_element_type=jnp.float32
    )
    col_width = observed.shape[1] // band_count
    offset = lax.axis_index("band") * col_width
    totals = lax.psum(partial_value, "band")
    full_rows = totals - observed.astype(jnp.float32)
    residual = lax.dynamic_slice_in_dim(full_rows, offset, col_width, 1)
    residual_rows = full_rows.astype(jnp.bfloat16)
    adjoint_part = jnp.einsum(
        "ukh,hs->uks", u_factors, residual_rows, preferred_element_type=jnp.float32
    )
    returned = lax.all_to_all(
        adjoint_part.astype(jnp.bfloat16), "tile", split_axis=0, concat_axis=0, tiled=True
    )
    summed = (
        returned.astype(jnp.float32)
        .reshape(row_tiles, slices_per, rank_max, returned.shape[2])
        .sum(axis=1)
    )
    adjoint = (summed * weight[:, :, None]).astype(jnp.bfloat16)
    gradient = jnp.einsum("ikb,iks->bs", v_factors, adjoint, preferred_element_type=jnp.float32)
    return (residual, gradient.astype(jnp.bfloat16))


def solution(mesh):
    in_specs = (
        P(("band", "tile"), None),
        P("tile", None),
        P(None, None, ("band", "tile")),
        P("band", None, "tile"),
        P(None, ("band", "tile")),
        P(None, ("band", "tile")),
        P(None, ("band", "tile")),
    )
    out_specs = (P("tile", "band"), P(("band", "tile"), None))
    return jax.shard_map(local, mesh=mesh, in_specs=in_specs, out_specs=out_specs, check_vma=False)
```

profile of v0, /device:TPU:4, one launch (start us, length us, event | category | flops | bytes accessed | tf_op | source)
XLA Modules:
  0.0 238.3 jit_solution(13547615035790127038)
XLA Ops:
  7.2 0.0 copy-start
  7.2 0.0 all-reduce.2.cloned.1.call-start
  7.2 0.8 exponential_bitcast_fusion
  8.0 0.7 fusion.8
  8.7 2.1 fusion.2
  10.8 0.2 broadcast_in_dim.2
  11.0 49.3 %all_to_all.10 = bf16[32,96,256]{2,1,0:T(8,128)(2,1)S(1)} all-to-all(bf16[32,96,256]{2,1,0:T(8,128)(2,1)S(1)} %bitcast.32), channel_id=1, replica_groups=mesh['band'=16,'tile'=32] {'tile'}, dimensions={0} | all-to-all | bytes 3145728 | tf_op jit(solution)/shard_map/all_to_all | solution.py:19
  60.3 0.0 copy-done
  60.3 0.0 copy-start.1
  60.3 1.3 convolution_bitcast_fusion.1
  61.7 0.0 all-reduce.2.cloned.1.call-update
  61.7 0.0 copy-done.1
  61.7 0.1 copy.9
  61.8 114.5 %all-reduce.2.cloned.1.call-done = f32[256,256]{0,1:T(8,128)} async-done(((f32[256,256]{0,1:T(8,128)}), f32[256,256]{0,1:T(8,128)}) %all-reduce.2.cloned.1.call-update) | async-done | bytes 262160 | tf_op jit(solution)/shard_map/psum | solution.py:25
  176.3 1.0 convert_subtract_fusion
  177.3 1.8 fusion
  179.1 9.9 %all-to-all-start.1 = ((bf16[32,96,256]{2,1,0:T(8,128)(2,1)}), bf16[32,96,256]{2,1,0:T(8,128)(2,1)S(1)}, u32[]{:S(2)}, u32[]{:S(2)}) async-start(bf16[32,96,256]{2,1,0:T(8,128)(2,1)} %fusion), calls=%async_computation.1 | async-start | bytes 3145728 | tf_op jit(solution)/shard_map/all_to_all | solution.py:32
  189.0 0.6 constant_dynamic-slice_fusion
  189.6 38.7 %all-to-all-done.1 = bf16[32,96,256]{2,1,0:T(8,128)(2,1)S(1)} async-done(((bf16[32,96,256]{2,1,0:T(8,128)(2,1)}), bf16[32,96,256]{2,1,0:T(8,128)(2,1)S(1)}, u32[]{:S(2)}, u32[]{:S(2)}) %all-to-all-start.1) | async-done | bytes 1572896 | tf_op jit(solution)/shard_map/all_to_all | solution.py:32
  228.3 0.0 copy-start.2
  228.3 0.2 convert_reduce_fusion
  228.5 1.2 copy-done.2
  229.7 0.7 fusion.3
  230.4 1.0 copy.11
Async XLA Ops:
  7.2 53.2 %copy-start = (bf16[32,96,256]{2,1,0:T(8,128)(2,1)S(1)}, bf16[32,96,256]{2,1,0:T(8,128)(2,1)}, u32[]{:S(2)}) copy-start(bf16[32,96,256]{2,1,0:T(8,128)(2,1)} %param.10) | copy-start | bytes 4718596
  7.2 169.2 %all-reduce.2.cloned.1.call-start = ((), (), s32[]{:S(2)}) async-start(), calls=%async_computation.2 | async-start | bytes 524288 | tf_op jit(solution)/shard_map/psum | solution.py:25
  60.3 1.3 copy-start.1
  179.1 49.2 %all-to-all-start.1 = ((bf16[32,96,256]{2,1,0:T(8,128)(2,1)}), bf16[32,96,256]{2,1,0:T(8,128)(2,1)S(1)}, u32[]{:S(2)}, u32[]{:S(2)}) async-start(bf16[32,96,256]{2,1,0:T(8,128)(2,1)} %fusion), calls=%async_computation.1 | async-start | bytes 3145728 | tf_op jit(solution)/shard_map/all_to_all | solution.py:32
  228.3 1.4 copy-start.2
Sparse Core Ops, SparseCore 0:
  61.8 114.4 all-reduce.1
where the time goes:
time: 239 us; the launch traced here: 238 us
  waiting for transfers between devices  153 us (64%)
  blocking collectives  49.3 us (21%)
  between operations  14.1 us (6%)
  starting transfers between devices  9.9 us (4%)
  matrix products  5.87 us (2%)
  local copies, waits for them, and re-layouts  3.08 us (1%)
  other arithmetic  2.71 us (1%)
    psum x1, waiting for transfers between devices, local(): totals = lax.psum(partial_value, 'band')  115 us
    all_to_all x1, blocking collectives, local(): lax.all_to_all(outgoing, 'tile', split_axis=0, concat_axis=0, tiled=True)  49.3 us
    all_to_all x1, waiting for transfers between devices, local(): lax.all_to_all(adjoint_part.astype(jnp.bfloat16), 'tile', split_axis=0, c...  38.7 us
    all_to_all x1, starting transfers between devices, local(): lax.all_to_all(adjoint_part.astype(jnp.bfloat16), 'tile', split_axis=0, c...  9.86 us
  transfers between devices with their start and end apart: 2, of which 2 were waited for; matrix products, arithmetic and copies ran while one was open for 0% of the time, Pallas kernels for 0%

commit v1 on v0

--- a/solution.py
+++ b/solution.py
@@ -22,7 +22,9 @@
     )
     col_width = observed.shape[1] // band_count
     offset = lax.axis_index("band") * col_width
-    totals = lax.psum(partial_value, "band")
+    totals = partial_value
+    for hop in (1, 2, 4, 8):
+        totals = totals + lax.ppermute(totals, "band", [(dev, dev ^ hop) for dev in range(16)])
     full_rows = totals - observed.astype(jnp.float32)
     residual = lax.dynamic_slice_in_dim(full_rows, offset, col_width, 1)
     residual_rows = full_rows.astype(jnp.bfloat16)

time: 239 us -> 154 us (0.64)
  the two profiles are of different devices: /device:TPU:4 before, /device:TPU:194 now
where the time goes in v1:
time: 154 us
  waiting for transfers between devices  74 us (48%)
  blocking collectives  49.4 us (32%)
  starting transfers between devices  19.7 us (13%)
  matrix products  5.15 us (3%)
  local copies, waits for them, and re-layouts  3.08 us (2%)
  other arithmetic  1.89 us (1%)
    all_to_all x1, blocking collectives, local(): lax.all_to_all(outgoing, 'tile', split_axis=0, concat_axis=0, tiled=True)  49.4 us
    all_to_all x1, waiting for transfers between devices, local(): lax.all_to_all(adjoint_part.astype(jnp.bfloat16), 'tile', split_axis=0, c...  38.2 us
    ppermute x4, waiting for transfers between devices, local(): lax.ppermute(totals, 'band', [(dev, dev ^ hop) for dev in range(16)])  35.8 us
    ppermute x4, starting transfers between devices, local(): lax.ppermute(totals, 'band', [(dev, dev ^ hop) for dev in range(16)])  14.1 us
    all_to_all x1, starting transfers between devices, local(): lax.all_to_all(adjoint_part.astype(jnp.bfloat16), 'tile', split_axis=0, c...  5.57 us
  transfers between devices with their start and end apart: 5, of which 5 were waited for; matrix products, arithmetic and copies ran while one was open for 0% of the time, Pallas kernels for 0%

profile of v1, /device:TPU:194, one launch (start us, length us, event | category | flops | bytes accessed | tf_op | source)
XLA Modules:
  0.0 154.0 jit_solution(17842790024862163306)
XLA Ops:
  0.6 0.0 copy-start
  0.6 0.8 exponential_bitcast_fusion
  1.4 0.7 fusion.8
  2.2 2.1 %fusion.2 = bf16[8,96,256]{2,1,0:T(8,128)(2,1)S(1)} fusion(bf16[8,96,1024]{2,1,0:T(8,128)(2,1)} %param.9, bf16[1024,256]{1,0:T(8,128)(2,1)} %param.7, f32[8,96]{1,0:T(8,128)S(1)} %fusion.8), kind=kOutput, calls=%fused_computation.6 | convolution fusion | flops 403046400 | bytes 2493440 | tf_op jit(solution)/shard_map/ikb,bs->iks/dot_general | solution.py:16
  4.3 0.2 broadcast_in_dim.2
  4.4 49.4 %all_to_all.10 = bf16[32,96,256]{2,1,0:T(8,128)(2,1)S(1)} all-to-all(bf16[32,96,256]{2,1,0:T(8,128)(2,1)S(1)} %bitcast.32), channel_id=1, replica_groups=mesh['band'=16,'tile'=32] {'tile'}, dimensions={0} | all-to-all | bytes 3145728 | tf_op jit(solution)/shard_map/all_to_all | solution.py:19
  53.8 0.0 copy-done
  53.8 0.6 convolution_bitcast_fusion.1
  54.4 0.0 copy-start.1
  54.4 2.1 %collective-permute-start = (f32[256,256]{0,1:T(8,128)S(1)}, f32[256,256]{0,1:T(8,128)S(1)}, u32[]{:S(2)}, u32[]{:S(2)}) collective-permute-start(f32[256,256]{0,1:T(8,128)S(1)} %convolution_bitcast_fusion.1), channel_id=1, source_target_pairs={{0,32},{32,0},{64,96},{96,64},{128,160},{160,128},{192,224},{224,1... | collective-permute-start | bytes 786440 | tf_op jit(solution)/shard_map/ppermute | solution.py:27
  56.5 1.5 collective-permute-done
  58.0 1.9 %collective-permute-start.1 = (f32[256,256]{0,1:T(8,128)S(1)}, f32[256,256]{0,1:T(8,128)S(1)}, u32[]{:S(2)}, u32[]{:S(2)}) collective-permute-start(f32[256,256]{0,1:T(8,128)S(1)} %add.19), channel_id=1, source_target_pairs={{0,64},{32,96},{64,0},{96,32},{128,192},{160,224},{192,128},{224,1... | collective-permute-start | bytes 786440 | tf_op jit(solution)/shard_map/ppermute | solution.py:27
  60.0 8.3 %collective-permute-done.1 = f32[256,256]{0,1:T(8,128)S(1)} collective-permute-done((f32[256,256]{0,1:T(8,128)S(1)}, f32[256,256]{0,1:T(8,128)S(1)}, u32[]{:S(2)}, u32[]{:S(2)}) %collective-permute-start.1) | collective-permute-done | bytes 262176 | tf_op jit(solution)/shard_map/ppermute | solution.py:27
  68.3 1.9 %collective-permute-start.2 = (f32[256,256]{0,1:T(8,128)S(1)}, f32[256,256]{0,1:T(8,128)S(1)}, u32[]{:S(2)}, u32[]{:S(2)}) collective-permute-start(f32[256,256]{0,1:T(8,128)S(1)} %add.20), channel_id=1, source_target_pairs={{0,128},{32,160},{64,192},{96,224},{128,0},{160,32},{192,64},{224,... | collective-permute-start | bytes 786440 | tf_op jit(solution)/shard_map/ppermute | solution.py:27
  70.2 14.0 %collective-permute-done.2 = f32[256,256]{0,1:T(8,128)S(1)} collective-permute-done((f32[256,256]{0,1:T(8,128)S(1)}, f32[256,256]{0,1:T(8,128)S(1)}, u32[]{:S(2)}, u32[]{:S(2)}) %collective-permute-start.2) | collective-permute-done | bytes 262176 | tf_op jit(solution)/shard_map/ppermute | solution.py:27
  84.3 8.3 %collective-permute-start.3 = (f32[256,256]{0,1:T(8,128)S(1)}, f32[256,256]{0,1:T(8,128)S(1)}, u32[]{:S(2)}, u32[]{:S(2)}) collective-permute-start(f32[256,256]{0,1:T(8,128)S(1)} %add.21), channel_id=1, source_target_pairs={{0,256},{32,288},{64,320},{96,352},{128,384},{160,416},{192,448},{... | collective-permute-start | bytes 786440 | tf_op jit(solution)/shard_map/ppermute | solution.py:27
  92.5 0.0 copy-done.1
  92.5 0.1 copy.9
  92.7 12.0 %collective-permute-done.3 = f32[256,256]{0,1:T(8,128)S(1)} collective-permute-done((f32[256,256]{0,1:T(8,128)S(1)}, f32[256,256]{0,1:T(8,128)S(1)}, u32[]{:S(2)}, u32[]{:S(2)}) %collective-permute-start.3) | collective-permute-done | bytes 262176 | tf_op jit(solution)/shard_map/ppermute | solution.py:27
  104.7 1.8 %fusion = bf16[32,96,256]{2,1,0:T(8,128)(2,1)} fusion(bf16[32,96,256]{2,1,0:T(8,128)(2,1)S(1)} %copy-done, f32[256,256]{0,1:T(8,128)S(1)} %convert_subtract_fusion), kind=kOutput, calls=%fused_computation.2 | convolution fusion | flops 403505152 | bytes 3407872 | tf_op jit(solution)/shard_map/ukh,hs->uks/dot_general | solution.py:31
  106.4 5.6 %all-to-all-start.1 = ((bf16[32,96,256]{2,1,0:T(8,128)(2,1)}), bf16[32,96,256]{2,1,0:T(8,128)(2,1)S(1)}, u32[]{:S(2)}, u32[]{:S(2)}) async-start(bf16[32,96,256]{2,1,0:T(8,128)(2,1)} %fusion), calls=%async_computation.1 | async-start | bytes 3145728 | tf_op jit(solution)/shard_map/all_to_all | solution.py:34
  112.0 0.6 constant_dynamic-slice_fusion
  112.6 38.2 %all-to-all-done.1 = bf16[32,96,256]{2,1,0:T(8,128)(2,1)S(1)} async-done(((bf16[32,96,256]{2,1,0:T(8,128)(2,1)}), bf16[32,96,256]{2,1,0:T(8,128)(2,1)S(1)}, u32[]{:S(2)}, u32[]{:S(2)}) %all-to-all-start.1) | async-done | bytes 1572896 | tf_op jit(solution)/shard_map/all_to_all | solution.py:34
  150.9 0.0 copy-start.2
  150.9 0.2 convert_reduce_fusion
  151.1 1.2 copy-done.2
  152.3 0.7 fusion.3
  153.0 1.0 copy.11
  (4 shorter events, 0.1 us)
Async XLA Ops:
  0.6 53.2 %copy-start = (bf16[32,96,256]{2,1,0:T(8,128)(2,1)S(1)}, bf16[32,96,256]{2,1,0:T(8,128)(2,1)}, u32[]{:S(2)}) copy-start(bf16[32,96,256]{2,1,0:T(8,128)(2,1)} %param.10) | copy-start | bytes 4718596
  54.4 38.1 %copy-start.1 = (bf16[256,256]{1,0:T(8,128)(2,1)S(1)}, bf16[256,256]{1,0:T(8,128)(2,1)}, u32[]{:S(2)}) copy-start(bf16[256,256]{1,0:T(8,128)(2,1)} %param.8) | copy-start | bytes 393220
  54.4 3.6 %collective-permute-start = (f32[256,256]{0,1:T(8,128)S(1)}, f32[256,256]{0,1:T(8,128)S(1)}, u32[]{:S(2)}, u32[]{:S(2)}) collective-permute-start(f32[256,256]{0,1:T(8,128)S(1)} %convolution_bitcast_fusion.1), channel_id=1, source_target_pairs={{0,32},{32,0},{64,96},{96,64},{128,160},{160,128},{192,224},{224,1... | collective-permute-start | bytes 786440 | tf_op jit(solution)/shard_map/ppermute | solution.py:27
  58.0 10.2 %collective-permute-start.1 = (f32[256,256]{0,1:T(8,128)S(1)}, f32[256,256]{0,1:T(8,128)S(1)}, u32[]{:S(2)}, u32[]{:S(2)}) collective-permute-start(f32[256,256]{0,1:T(8,128)S(1)} %add.19), channel_id=1, source_target_pairs={{0,64},{32,96},{64,0},{96,32},{128,192},{160,224},{192,128},{224,1... | collective-permute-start | bytes 786440 | tf_op jit(solution)/shard_map/ppermute | solution.py:27
  68.3 15.9 %collective-permute-start.2 = (f32[256,256]{0,1:T(8,128)S(1)}, f32[256,256]{0,1:T(8,128)S(1)}, u32[]{:S(2)}, u32[]{:S(2)}) collective-permute-start(f32[256,256]{0,1:T(8,128)S(1)} %add.20), channel_id=1, source_target_pairs={{0,128},{32,160},{64,192},{96,224},{128,0},{160,32},{192,64},{224,... | collective-permute-start | bytes 786440 | tf_op jit(solution)/shard_map/ppermute | solution.py:27
  84.3 20.4 %collective-permute-start.3 = (f32[256,256]{0,1:T(8,128)S(1)}, f32[256,256]{0,1:T(8,128)S(1)}, u32[]{:S(2)}, u32[]{:S(2)}) collective-permute-start(f32[256,256]{0,1:T(8,128)S(1)} %add.21), channel_id=1, source_target_pairs={{0,256},{32,288},{64,320},{96,352},{128,384},{160,416},{192,448},{... | collective-permute-start | bytes 786440 | tf_op jit(solution)/shard_map/ppermute | solution.py:27
  106.4 44.4 %all-to-all-start.1 = ((bf16[32,96,256]{2,1,0:T(8,128)(2,1)}), bf16[32,96,256]{2,1,0:T(8,128)(2,1)S(1)}, u32[]{:S(2)}, u32[]{:S(2)}) async-start(bf16[32,96,256]{2,1,0:T(8,128)(2,1)} %fusion), calls=%async_computation.1 | async-start | bytes 3145728 | tf_op jit(solution)/shard_map/all_to_all | solution.py:34
  150.9 1.4 copy-start.2
